TPU v7x, 128 devices: a whole 4x4x4 slice. The times are simulated.
128 devices in a mesh: aux: 16 (over z_lo, x, core), orb: 8 (over y, z_hi).
Axes of the slice: x: 4, y: 4, z: 4 (z_hi: 2, z_lo: 2; z = z_hi * 2 + z_lo), core: 2. Of those that a mesh axis runs over, the one named last changes fastest.
Arguments:
- b_factors: float32 [16, 1024, 20480], P('aux', None, 'orb'), may hold values from -6 to 6
- occupied: float32 [20480, 2048], P('orb', 'aux'), may hold values from -0.0390625 to 0.0390625
- b_mask: int32 [16, 8, 160], P('aux', None, 'orb'), may hold values 0 or 1
- c_mask: int32 [160, 16], P('orb', 'aux'), may hold values 0 or 1
Outputs:
- exchange: float32 [1024, 1024], P('orb')
All inputs are finite; a program needn't handle non-finite values. No bound on the sum of `b_mask` or of `c_mask` on one device may be relied on, other than what follows from the above.
Results may differ from a plain program's by a relative error of at most 0.0001.
Values sent between devices are 32-bit elements; how exact they have to be, the bound alone decides.
No kernel may reach another device: no remote copies, remote signals or barrier semaphores. Data moves between devices by JAX's collectives and lax.ppermute only.
A program may use at most 128 MiB of HBM per device.

v0:
```python
import math

import jax
import jax.numpy as jnp
from jax import lax
from jax.sharding import PartitionSpec as P

BLK = 128
NOCC = 2048


def shifted(value, axis, steps):
    count = lax.axis_size(axis)
    pairs = [(source, (source + steps) % count) for source in range(count)]
    return lax.ppermute(value, axis, pairs)


def expand(mask_blocks):
    spread = jnp.repeat(mask_blocks.astype(jnp.float32), BLK, axis=-2)
    return jnp.repeat(spread, BLK, axis=-1)


def body(b_factors, occupied, b_mask, c_mask):
    masked_factors = b_factors * expand(b_mask)
    panel_now = occupied * expand(c_mask)
    naux_dev = lax.axis_size("aux")
    norb_dev = lax.axis_size("orb")
    myself = lax.axis_index("aux")
    width = panel_now.shape[1]
    fitted = jnp.zeros(
        (masked_factors.shape[0], masked_factors.shape[1], width * naux_dev), jnp.float32
    )

    def transform(panel):
        return jnp.einsum("qml,li->qmi", masked_factors, panel, precision=lax.Precision.HIGHEST)

    def insert(target, panel, source):
        source = jnp.mod(source, naux_dev)
        return lax.dynamic_update_slice(
            target, transform(panel), (jnp.int32(0), jnp.int32(0), source * width)
        )

    fitted = insert(fitted, panel_now, myself)

    def advance(turn_index, carried):
        panel, target = carried
        panel = shifted(panel, "aux", 1)
        return (panel, insert(target, panel, myself - turn_index))

    unused, fitted = lax.fori_loop(1, naux_dev, advance, (panel_now, fitted))
    row_count = fitted.shape[1] // norb_dev
    factor = 1.0 / math.sqrt(masked_factors.shape[0] * naux_dev * NOCC)
    summed = lax.psum(fitted, "orb")
    own_rows = lax.dynamic_slice_in_dim(summed, lax.axis_index("orb") * row_count, row_count, 1)
    partial_rows = jnp.einsum("qmi,qni->mn", own_rows, summed, precision=lax.Precision.HIGHEST)
    kblock = lax.psum(partial_rows, "aux")
    return kblock * factor


def solution(mesh):
    placed = (P("aux", None, "orb"), P("orb", "aux"), P("aux", None, "orb"), P("orb", "aux"))
    return jax.shard_map(
        body, mesh=mesh, in_specs=placed, out_specs=P("orb", None), check_vma=False
    )
```

profile of v0, /device:TPU:1, one launch (start us, length us, event | category | flops | bytes accessed | tf_op | source)
XLA Modules:
  0.0 1015.2 jit_solution(6916626476184319603)
XLA Ops:
  6.5 11.4 %copy.6 = f32[1,1024,2560]{1,2,0:T(8,128)} copy(f32[1,1024,2560]{2,1,0:T(8,128)} %param.6) | data formatting | bytes 20971520 | tf_op args[0]
  18.0 0.1 copy.5
  18.3 10.3 %bitcast_multiply_fusion = f32[1,1024,2560]{1,2,0:T(8,128)} fusion(f32[1,1024,2560]{1,2,0:T(8,128)} %copy.6, f32[1024,20]{0,1:T(8,128)S(1)} %bitcast.50), kind=kLoop, calls=%fused_computation.6 | loop fusion | flops 2621440 | bytes 21053440 | tf_op jit(solution)/shard_map/mul | solution.py:24
  28.6 11.6 %copy.7 = f32[1,1024,2560]{2,1,0:T(8,128)} copy(f32[1,1024,2560]{1,2,0:T(8,128)} %bitcast_multiply_fusion) | data formatting | bytes 20971520 | tf_op jit(solution)/shard_map/while | solution.py:50
  40.2 0.4 broadcast_multiply_fusion
  40.6 1.0 broadcast_in_dim.21
  41.6 2.5 copy-done
  44.2 16.6 %fusion.15 = f32[1,1024,2048]{2,1,0:T(8,128)S(1)} fusion(f32[1,1024,2048]{2,1,0:T(8,128)S(1)} %broadcast_in_dim.21, s32[]{:T(128)S(6)} %select_n.41, f32[2560,128]{1,0:T(8,128)S(1)} %broadcast_multiply_fusion, f32[1,1024,2560]{1,2,0:T(8,128)S(1)} %copy-done), kind=kOutput, calls=%fused_computation.10 | convolution fusion | flops 4026531840 | bytes 12320772 | tf_op jit(solution)/shard_map/qml,li->qmi/dot_general | solution.py:35
  60.8 3.3 copy-done.1
  64.1 448.8 %while.17 = (s32[]{:T(128)}, f32[2560,128]{1,0:T(8,128)S(1)}, f32[1,1024,2048]{2,1,0:T(8,128)}, f32[1,1024,2560]{2,1,0:T(8,128)}, s32[]{:T(128)}, /*index=5*/s32...) while((s32[]{:T(128)}, f32[2560,128]{1,0:T(8,128)S(1)}, ...), condition=%wide.region_1.2_spmd, body=%wide.region_0.1_spmd.sunk | while | flops 4026531840 | bytes 20185408 | solution.py:50
  64.1 2.6 collective-permute-start
  66.7 14.6 %collective-permute-done = f32[2560,128]{1,0:T(8,128)S(1)} collective-permute-done((f32[2560,128]{1,0:T(8,128)S(1)}, f32[2560,128]{1,0:T(8,128)S(1)}, u32[]{:S(2)}, u32[]{:S(2)}) %collective-permute-start) | collective-permute-done | bytes 1310752 | tf_op jit(solution)/shard_map/while/body/eval_jaxpr/ppermute | solution.py:15
  81.2 0.1 copy.18
  81.3 11.7 %fusion.28 = f32[1,1024,2048]{2,1,0:T(8,128)} fusion(f32[1,1024,2048]{2,1,0:T(8,128)} %get-tuple-element.198, s32[]{:T(128)S(6)} %select_n.46, f32[2560,128]{1,0:T(8,128)S(1)} %collective-permute-done, f32[1,1024,2560]{2,1,0:T(8,128)} %get-tuple-element.210), kind=kOutput, calls=%fused_computation.3.clone.1 | convolution fusion | flops 4026531840 | bytes 12320772 | tf_op jit(solution)/shard_map/while/body/eval_jaxpr/qml,li->qmi/dot_general | solution.py:35
  93.0 2.5 collective-permute-start
  95.5 14.6 %collective-permute-done = f32[2560,128]{1,0:T(8,128)S(1)} collective-permute-done((f32[2560,128]{1,0:T(8,128)S(1)}, f32[2560,128]{1,0:T(8,128)S(1)}, u32[]{:S(2)}, u32[]{:S(2)}) %collective-permute-start) | collective-permute-done | bytes 1310752 | tf_op jit(solution)/shard_map/while/body/eval_jaxpr/ppermute | solution.py:15
  110.1 0.1 copy.18
  110.2 11.7 %fusion.28 = f32[1,1024,2048]{2,1,0:T(8,128)} fusion(f32[1,1024,2048]{2,1,0:T(8,128)} %get-tuple-element.198, s32[]{:T(128)S(6)} %select_n.46, f32[2560,128]{1,0:T(8,128)S(1)} %collective-permute-done, f32[1,1024,2560]{2,1,0:T(8,128)} %get-tuple-element.210), kind=kOutput, calls=%fused_computation.3.clone.1 | convolution fusion | flops 4026531840 | bytes 12320772 | tf_op jit(solution)/shard_map/while/body/eval_jaxpr/qml,li->qmi/dot_general | solution.py:35
  121.9 2.5 collective-permute-start
  124.3 14.6 %collective-permute-done = f32[2560,128]{1,0:T(8,128)S(1)} collective-permute-done((f32[2560,128]{1,0:T(8,128)S(1)}, f32[2560,128]{1,0:T(8,128)S(1)}, u32[]{:S(2)}, u32[]{:S(2)}) %collective-permute-start) | collective-permute-done | bytes 1310752 | tf_op jit(solution)/shard_map/while/body/eval_jaxpr/ppermute | solution.py:15
  138.9 0.1 copy.18
  139.0 11.7 %fusion.28 = f32[1,1024,2048]{2,1,0:T(8,128)} fusion(f32[1,1024,2048]{2,1,0:T(8,128)} %get-tuple-element.198, s32[]{:T(128)S(6)} %select_n.46, f32[2560,128]{1,0:T(8,128)S(1)} %collective-permute-done, f32[1,1024,2560]{2,1,0:T(8,128)} %get-tuple-element.210), kind=kOutput, calls=%fused_computation.3.clone.1 | convolution fusion | flops 4026531840 | bytes 12320772 | tf_op jit(solution)/shard_map/while/body/eval_jaxpr/qml,li->qmi/dot_general | solution.py:35
  150.7 2.5 collective-permute-start
  153.2 14.6 %collective-permute-done = f32[2560,128]{1,0:T(8,128)S(1)} collective-permute-done((f32[2560,128]{1,0:T(8,128)S(1)}, f32[2560,128]{1,0:T(8,128)S(1)}, u32[]{:S(2)}, u32[]{:S(2)}) %collective-permute-start) | collective-permute-done | bytes 1310752 | tf_op jit(solution)/shard_map/while/body/eval_jaxpr/ppermute | solution.py:15
  167.7 0.1 copy.18
  167.8 11.7 %fusion.28 = f32[1,1024,2048]{2,1,0:T(8,128)} fusion(f32[1,1024,2048]{2,1,0:T(8,128)} %get-tuple-element.198, s32[]{:T(128)S(6)} %select_n.46, f32[2560,128]{1,0:T(8,128)S(1)} %collective-permute-done, f32[1,1024,2560]{2,1,0:T(8,128)} %get-tuple-element.210), kind=kOutput, calls=%fused_computation.3.clone.1 | convolution fusion | flops 4026531840 | bytes 12320772 | tf_op jit(solution)/shard_map/while/body/eval_jaxpr/qml,li->qmi/dot_general | solution.py:35
  179.5 2.5 collective-permute-start
  182.0 14.6 %collective-permute-done = f32[2560,128]{1,0:T(8,128)S(1)} collective-permute-done((f32[2560,128]{1,0:T(8,128)S(1)}, f32[2560,128]{1,0:T(8,128)S(1)}, u32[]{:S(2)}, u32[]{:S(2)}) %collective-permute-start) | collective-permute-done | bytes 1310752 | tf_op jit(solution)/shard_map/while/body/eval_jaxpr/ppermute | solution.py:15
  196.6 0.1 copy.18
  196.7 11.7 %fusion.28 = f32[1,1024,2048]{2,1,0:T(8,128)} fusion(f32[1,1024,2048]{2,1,0:T(8,128)} %get-tuple-element.198, s32[]{:T(128)S(6)} %select_n.46, f32[2560,128]{1,0:T(8,128)S(1)} %collective-permute-done, f32[1,1024,2560]{2,1,0:T(8,128)} %get-tuple-element.210), kind=kOutput, calls=%fused_computation.3.clone.1 | convolution fusion | flops 4026531840 | bytes 12320772 | tf_op jit(solution)/shard_map/while/body/eval_jaxpr/qml,li->qmi/dot_general | solution.py:35
  208.3 2.5 collective-permute-start
  210.8 14.6 %collective-permute-done = f32[2560,128]{1,0:T(8,128)S(1)} collective-permute-done((f32[2560,128]{1,0:T(8,128)S(1)}, f32[2560,128]{1,0:T(8,128)S(1)}, u32[]{:S(2)}, u32[]{:S(2)}) %collective-permute-start) | collective-permute-done | bytes 1310752 | tf_op jit(solution)/shard_map/while/body/eval_jaxpr/ppermute | solution.py:15
  225.4 0.1 copy.18
  225.5 11.7 %fusion.28 = f32[1,1024,2048]{2,1,0:T(8,128)} fusion(f32[1,1024,2048]{2,1,0:T(8,128)} %get-tuple-element.198, s32[]{:T(128)S(6)} %select_n.46, f32[2560,128]{1,0:T(8,128)S(1)} %collective-permute-done, f32[1,1024,2560]{2,1,0:T(8,128)} %get-tuple-element.210), kind=kOutput, calls=%fused_computation.3.clone.1 | convolution fusion | flops 4026531840 | bytes 12320772 | tf_op jit(solution)/shard_map/while/body/eval_jaxpr/qml,li->qmi/dot_general | solution.py:35
  237.2 2.4 collective-permute-start
  239.7 14.6 %collective-permute-done = f32[2560,128]{1,0:T(8,128)S(1)} collective-permute-done((f32[2560,128]{1,0:T(8,128)S(1)}, f32[2560,128]{1,0:T(8,128)S(1)}, u32[]{:S(2)}, u32[]{:S(2)}) %collective-permute-start) | collective-permute-done | bytes 1310752 | tf_op jit(solution)/shard_map/while/body/eval_jaxpr/ppermute | solution.py:15
  254.2 0.1 copy.18
  254.3 11.7 %fusion.28 = f32[1,1024,2048]{2,1,0:T(8,128)} fusion(f32[1,1024,2048]{2,1,0:T(8,128)} %get-tuple-element.198, s32[]{:T(128)S(6)} %select_n.46, f32[2560,128]{1,0:T(8,128)S(1)} %collective-permute-done, f32[1,1024,2560]{2,1,0:T(8,128)} %get-tuple-element.210), kind=kOutput, calls=%fused_computation.3.clone.1 | convolution fusion | flops 4026531840 | bytes 12320772 | tf_op jit(solution)/shard_map/while/body/eval_jaxpr/qml,li->qmi/dot_general | solution.py:35
  266.0 2.5 collective-permute-start
  268.5 16.1 %collective-permute-done = f32[2560,128]{1,0:T(8,128)S(1)} collective-permute-done((f32[2560,128]{1,0:T(8,128)S(1)}, f32[2560,128]{1,0:T(8,128)S(1)}, u32[]{:S(2)}, u32[]{:S(2)}) %collective-permute-start) | collective-permute-done | bytes 1310752 | tf_op jit(solution)/shard_map/while/body/eval_jaxpr/ppermute | solution.py:15
  284.6 0.1 copy.18
  284.7 11.7 %fusion.28 = f32[1,1024,2048]{2,1,0:T(8,128)} fusion(f32[1,1024,2048]{2,1,0:T(8,128)} %get-tuple-element.198, s32[]{:T(128)S(6)} %select_n.46, f32[2560,128]{1,0:T(8,128)S(1)} %collective-permute-done, f32[1,1024,2560]{2,1,0:T(8,128)} %get-tuple-element.210), kind=kOutput, calls=%fused_computation.3.clone.1 | convolution fusion | flops 4026531840 | bytes 12320772 | tf_op jit(solution)/shard_map/while/body/eval_jaxpr/qml,li->qmi/dot_general | solution.py:35
  296.4 1.0 collective-permute-start
  297.3 18.2 %collective-permute-done = f32[2560,128]{1,0:T(8,128)S(1)} collective-permute-done((f32[2560,128]{1,0:T(8,128)S(1)}, f32[2560,128]{1,0:T(8,128)S(1)}, u32[]{:S(2)}, u32[]{:S(2)}) %collective-permute-start) | collective-permute-done | bytes 1310752 | tf_op jit(solution)/shard_map/while/body/eval_jaxpr/ppermute | solution.py:15
  315.6 11.7 %fusion.28 = f32[1,1024,2048]{2,1,0:T(8,128)} fusion(f32[1,1024,2048]{2,1,0:T(8,128)} %get-tuple-element.198, s32[]{:T(128)S(6)} %select_n.46, f32[2560,128]{1,0:T(8,128)S(1)} %collective-permute-done, f32[1,1024,2560]{2,1,0:T(8,128)} %get-tuple-element.210), kind=kOutput, calls=%fused_computation.3.clone.1 | convolution fusion | flops 4026531840 | bytes 12320772 | tf_op jit(solution)/shard_map/while/body/eval_jaxpr/qml,li->qmi/dot_general | solution.py:35
  327.3 19.1 %collective-permute-done = f32[2560,128]{1,0:T(8,128)S(1)} collective-permute-done((f32[2560,128]{1,0:T(8,128)S(1)}, f32[2560,128]{1,0:T(8,128)S(1)}, u32[]{:S(2)}, u32[]{:S(2)}) %collective-permute-start) | collective-permute-done | bytes 1310752 | tf_op jit(solution)/shard_map/while/body/eval_jaxpr/ppermute | solution.py:15
  346.6 11.7 %fusion.28 = f32[1,1024,2048]{2,1,0:T(8,128)} fusion(f32[1,1024,2048]{2,1,0:T(8,128)} %get-tuple-element.198, s32[]{:T(128)S(6)} %select_n.46, f32[2560,128]{1,0:T(8,128)S(1)} %collective-permute-done, f32[1,1024,2560]{2,1,0:T(8,128)} %get-tuple-element.210), kind=kOutput, calls=%fused_computation.3.clone.1 | convolution fusion | flops 4026531840 | bytes 12320772 | tf_op jit(solution)/shard_map/while/body/eval_jaxpr/qml,li->qmi/dot_general | solution.py:35
  358.3 19.1 %collective-permute-done = f32[2560,128]{1,0:T(8,128)S(1)} collective-permute-done((f32[2560,128]{1,0:T(8,128)S(1)}, f32[2560,128]{1,0:T(8,128)S(1)}, u32[]{:S(2)}, u32[]{:S(2)}) %collective-permute-start) | collective-permute-done | bytes 1310752 | tf_op jit(solution)/shard_map/while/body/eval_jaxpr/ppermute | solution.py:15
  377.5 11.7 %fusion.28 = f32[1,1024,2048]{2,1,0:T(8,128)} fusion(f32[1,1024,2048]{2,1,0:T(8,128)} %get-tuple-element.198, s32[]{:T(128)S(6)} %select_n.46, f32[2560,128]{1,0:T(8,128)S(1)} %collective-permute-done, f32[1,1024,2560]{2,1,0:T(8,128)} %get-tuple-element.210), kind=kOutput, calls=%fused_computation.3.clone.1 | convolution fusion | flops 4026531840 | bytes 12320772 | tf_op jit(solution)/shard_map/while/body/eval_jaxpr/qml,li->qmi/dot_general | solution.py:35
  389.2 19.1 %collective-permute-done = f32[2560,128]{1,0:T(8,128)S(1)} collective-permute-done((f32[2560,128]{1,0:T(8,128)S(1)}, f32[2560,128]{1,0:T(8,128)S(1)}, u32[]{:S(2)}, u32[]{:S(2)}) %collective-permute-start) | collective-permute-done | bytes 1310752 | tf_op jit(solution)/shard_map/while/body/eval_jaxpr/ppermute | solution.py:15
  408.4 11.7 %fusion.28 = f32[1,1024,2048]{2,1,0:T(8,128)} fusion(f32[1,1024,2048]{2,1,0:T(8,128)} %get-tuple-element.198, s32[]{:T(128)S(6)} %select_n.46, f32[2560,128]{1,0:T(8,128)S(1)} %collective-permute-done, f32[1,1024,2560]{2,1,0:T(8,128)} %get-tuple-element.210), kind=kOutput, calls=%fused_computation.3.clone.1 | convolution fusion | flops 4026531840 | bytes 12320772 | tf_op jit(solution)/shard_map/while/body/eval_jaxpr/qml,li->qmi/dot_general | solution.py:35
  420.1 19.1 %collective-permute-done = f32[2560,128]{1,0:T(8,128)S(1)} collective-permute-done((f32[2560,128]{1,0:T(8,128)S(1)}, f32[2560,128]{1,0:T(8,128)S(1)}, u32[]{:S(2)}, u32[]{:S(2)}) %collective-permute-start) | collective-permute-done | bytes 1310752 | tf_op jit(solution)/shard_map/while/body/eval_jaxpr/ppermute | solution.py:15
  439.3 0.1 copy.18
  439.3 11.7 %fusion.28 = f32[1,1024,2048]{2,1,0:T(8,128)} fusion(f32[1,1024,2048]{2,1,0:T(8,128)} %get-tuple-element.198, s32[]{:T(128)S(6)} %select_n.46, f32[2560,128]{1,0:T(8,128)S(1)} %collective-permute-done, f32[1,1024,2560]{2,1,0:T(8,128)} %get-tuple-element.210), kind=kOutput, calls=%fused_computation.3.clone.1 | convolution fusion | flops 4026531840 | bytes 12320772 | tf_op jit(solution)/shard_map/while/body/eval_jaxpr/qml,li->qmi/dot_general | solution.py:35
  451.0 19.1 %collective-permute-done = f32[2560,128]{1,0:T(8,128)S(1)} collective-permute-done((f32[2560,128]{1,0:T(8,128)S(1)}, f32[2560,128]{1,0:T(8,128)S(1)}, u32[]{:S(2)}, u32[]{:S(2)}) %collective-permute-start) | collective-permute-done | bytes 1310752 | tf_op jit(solution)/shard_map/while/body/eval_jaxpr/ppermute | solution.py:15
  470.3 11.7 %fusion.28 = f32[1,1024,2048]{2,1,0:T(8,128)} fusion(f32[1,1024,2048]{2,1,0:T(8,128)} %get-tuple-element.198, s32[]{:T(128)S(6)} %select_n.46, f32[2560,128]{1,0:T(8,128)S(1)} %collective-permute-done, f32[1,1024,2560]{2,1,0:T(8,128)} %get-tuple-element.210), kind=kOutput, calls=%fused_computation.3.clone.1 | convolution fusion | flops 4026531840 | bytes 12320772 | tf_op jit(solution)/shard_map/while/body/eval_jaxpr/qml,li->qmi/dot_general | solution.py:35
  482.0 19.1 %collective-permute-done = f32[2560,128]{1,0:T(8,128)S(1)} collective-permute-done((f32[2560,128]{1,0:T(8,128)S(1)}, f32[2560,128]{1,0:T(8,128)S(1)}, u32[]{:S(2)}, u32[]{:S(2)}) %collective-permute-start) | collective-permute-done | bytes 1310752 | tf_op jit(solution)/shard_map/while/body/eval_jaxpr/ppermute | solution.py:15
  501.1 0.1 copy.18
  501.2 11.7 %fusion.28 = f32[1,1024,2048]{2,1,0:T(8,128)} fusion(f32[1,1024,2048]{2,1,0:T(8,128)} %get-tuple-element.198, s32[]{:T(128)S(6)} %select_n.46, f32[2560,128]{1,0:T(8,128)S(1)} %collective-permute-done, f32[1,1024,2560]{2,1,0:T(8,128)} %get-tuple-element.210), kind=kOutput, calls=%fused_computation.3.clone.1 | convolution fusion | flops 4026531840 | bytes 12320772 | tf_op jit(solution)/shard_map/while/body/eval_jaxpr/qml,li->qmi/dot_general | solution.py:35
  512.9 0.3 all-reduce.5.cloned.1.call-start
  513.2 357.9 %all-reduce.3.cloned.1.call-done = f32[1,1024,2048]{2,1,0:T(8,128)} async-done(((f32[1,1024,2048]{2,1,0:T(8,128)}), f32[1,1024,2048]{2,1,0:T(8,128)}) %all-reduce.3.cloned.1.call-update) | async-done | bytes 8388624 | tf_op jit(solution)/shard_map/psum | solution.py:53
  871.1 13.2 %fusion.10 = f32[128,1024]{1,0:T(8,128)} fusion(f32[1,1024,2048]{2,1,0:T(8,128)} %all-reduce.3.cloned.1.call-done, s32[]{:T(128)S(6)} %select_n.42), kind=kOutput, calls=%fused_computation.7 | convolution fusion | flops 3221225472 | bytes 9961476 | tf_op jit(solution)/shard_map/qmi,qni->mn/dot_general | solution.py:55
  884.3 122.2 %all-reduce.5.cloned.1.call-done = f32[128,1024]{1,0:T(8,128)} async-done(((f32[128,1024]{1,0:T(8,128)}), f32[128,1024]{1,0:T(8,128)}) %all-reduce.5.cloned.1.call-update) | async-done | bytes 524304 | tf_op jit(solution)/shard_map/psum | solution.py:56
  1006.5 1.9 broadcast_multiply_fusion.1
  (28 shorter events, 0.7 us)
Async XLA Ops:
  6.5 864.6 %all-reduce.3.cloned.1.call-start = ((), (), s32[]{:S(2)}) async-start(), calls=%async_computation | async-start | bytes 16777216 | tf_op jit(solution)/shard_map/psum | solution.py:53
  6.5 11.4 %copy-start.3 = (s32[1,8,20]{2,1,0:T(8,128)S(1)}, s32[1,8,20]{2,1,0:T(8,128)}, u32[]{:S(2)}) copy-start(s32[1,8,20]{2,1,0:T(8,128)} %param.8) | copy-start | bytes 1924
  6.5 11.7 %copy-start.4 = (s32[20,1]{0,1:T(1,128)S(1)}, s32[20,1]{0,1:T(1,128)}, u32[]{:S(2)}) copy-start(s32[20,1]{0,1:T(1,128)} %param.9) | copy-start | bytes 244
  28.6 11.6 %copy-start.2 = (f32[2560,128]{1,0:T(8,128)S(1)}, f32[2560,128]{1,0:T(8,128)}, u32[]{:S(2)}) copy-start(f32[2560,128]{1,0:T(8,128)} %param.7) | copy-start | bytes 3932164
  40.2 4.0 copy-start
  60.8 3.3 copy-start.1
  64.1 17.2 %collective-permute-start = (f32[2560,128]{1,0:T(8,128)S(1)}, f32[2560,128]{1,0:T(8,128)S(1)}, u32[]{:S(2)}, u32[]{:S(2)}) collective-permute-start(f32[2560,128]{1,0:T(8,128)S(1)} %get-tuple-element.197), channel_id=1, source_target_pairs={{0,8},{8,16},{16,24},{24,32},{32,40},{40,48},{48,56},{56,64},{64,7... | collective-permute-start | bytes 3932168 | tf_op jit(solution)/shard_map/while/body/eval_jaxpr/ppermute | solution.py:15
  93.0 17.0 %collective-permute-start = (f32[2560,128]{1,0:T(8,128)S(1)}, f32[2560,128]{1,0:T(8,128)S(1)}, u32[]{:S(2)}, u32[]{:S(2)}) collective-permute-start(f32[2560,128]{1,0:T(8,128)S(1)} %get-tuple-element.197), channel_id=1, source_target_pairs={{0,8},{8,16},{16,24},{24,32},{32,40},{40,48},{48,56},{56,64},{64,7... | collective-permute-start | bytes 3932168 | tf_op jit(solution)/shard_map/while/body/eval_jaxpr/ppermute | solution.py:15
  121.9 17.0 %collective-permute-start = (f32[2560,128]{1,0:T(8,128)S(1)}, f32[2560,128]{1,0:T(8,128)S(1)}, u32[]{:S(2)}, u32[]{:S(2)}) collective-permute-start(f32[2560,128]{1,0:T(8,128)S(1)} %get-tuple-element.197), channel_id=1, source_target_pairs={{0,8},{8,16},{16,24},{24,32},{32,40},{40,48},{48,56},{56,64},{64,7... | collective-permute-start | bytes 3932168 | tf_op jit(solution)/shard_map/while/body/eval_jaxpr/ppermute | solution.py:15
  150.7 17.0 %collective-permute-start = (f32[2560,128]{1,0:T(8,128)S(1)}, f32[2560,128]{1,0:T(8,128)S(1)}, u32[]{:S(2)}, u32[]{:S(2)}) collective-permute-start(f32[2560,128]{1,0:T(8,128)S(1)} %get-tuple-element.197), channel_id=1, source_target_pairs={{0,8},{8,16},{16,24},{24,32},{32,40},{40,48},{48,56},{56,64},{64,7... | collective-permute-start | bytes 3932168 | tf_op jit(solution)/shard_map/while/body/eval_jaxpr/ppermute | solution.py:15
  179.5 17.0 %collective-permute-start = (f32[2560,128]{1,0:T(8,128)S(1)}, f32[2560,128]{1,0:T(8,128)S(1)}, u32[]{:S(2)}, u32[]{:S(2)}) collective-permute-start(f32[2560,128]{1,0:T(8,128)S(1)} %get-tuple-element.197), channel_id=1, source_target_pairs={{0,8},{8,16},{16,24},{24,32},{32,40},{40,48},{48,56},{56,64},{64,7... | collective-permute-start | bytes 3932168 | tf_op jit(solution)/shard_map/while/body/eval_jaxpr/ppermute | solution.py:15
  208.3 17.1 %collective-permute-start = (f32[2560,128]{1,0:T(8,128)S(1)}, f32[2560,128]{1,0:T(8,128)S(1)}, u32[]{:S(2)}, u32[]{:S(2)}) collective-permute-start(f32[2560,128]{1,0:T(8,128)S(1)} %get-tuple-element.197), channel_id=1, source_target_pairs={{0,8},{8,16},{16,24},{24,32},{32,40},{40,48},{48,56},{56,64},{64,7... | collective-permute-start | bytes 3932168 | tf_op jit(solution)/shard_map/while/body/eval_jaxpr/ppermute | solution.py:15
  237.2 17.0 %collective-permute-start = (f32[2560,128]{1,0:T(8,128)S(1)}, f32[2560,128]{1,0:T(8,128)S(1)}, u32[]{:S(2)}, u32[]{:S(2)}) collective-permute-start(f32[2560,128]{1,0:T(8,128)S(1)} %get-tuple-element.197), channel_id=1, source_target_pairs={{0,8},{8,16},{16,24},{24,32},{32,40},{40,48},{48,56},{56,64},{64,7... | collective-permute-start | bytes 3932168 | tf_op jit(solution)/shard_map/while/body/eval_jaxpr/ppermute | solution.py:15
  266.0 18.6 %collective-permute-start = (f32[2560,128]{1,0:T(8,128)S(1)}, f32[2560,128]{1,0:T(8,128)S(1)}, u32[]{:S(2)}, u32[]{:S(2)}) collective-permute-start(f32[2560,128]{1,0:T(8,128)S(1)} %get-tuple-element.197), channel_id=1, source_target_pairs={{0,8},{8,16},{16,24},{24,32},{32,40},{40,48},{48,56},{56,64},{64,7... | collective-permute-start | bytes 3932168 | tf_op jit(solution)/shard_map/while/body/eval_jaxpr/ppermute | solution.py:15
  296.4 19.2 %collective-permute-start = (f32[2560,128]{1,0:T(8,128)S(1)}, f32[2560,128]{1,0:T(8,128)S(1)}, u32[]{:S(2)}, u32[]{:S(2)}) collective-permute-start(f32[2560,128]{1,0:T(8,128)S(1)} %get-tuple-element.197), channel_id=1, source_target_pairs={{0,8},{8,16},{16,24},{24,32},{32,40},{40,48},{48,56},{56,64},{64,7... | collective-permute-start | bytes 3932168 | tf_op jit(solution)/shard_map/while/body/eval_jaxpr/ppermute | solution.py:15
  327.3 19.2 %collective-permute-start = (f32[2560,128]{1,0:T(8,128)S(1)}, f32[2560,128]{1,0:T(8,128)S(1)}, u32[]{:S(2)}, u32[]{:S(2)}) collective-permute-start(f32[2560,128]{1,0:T(8,128)S(1)} %get-tuple-element.197), channel_id=1, source_target_pairs={{0,8},{8,16},{16,24},{24,32},{32,40},{40,48},{48,56},{56,64},{64,7... | collective-permute-start | bytes 3932168 | tf_op jit(solution)/shard_map/while/body/eval_jaxpr/ppermute | solution.py:15
  358.3 19.1 %collective-permute-start = (f32[2560,128]{1,0:T(8,128)S(1)}, f32[2560,128]{1,0:T(8,128)S(1)}, u32[]{:S(2)}, u32[]{:S(2)}) collective-permute-start(f32[2560,128]{1,0:T(8,128)S(1)} %get-tuple-element.197), channel_id=1, source_target_pairs={{0,8},{8,16},{16,24},{24,32},{32,40},{40,48},{48,56},{56,64},{64,7... | collective-permute-start | bytes 3932168 | tf_op jit(solution)/shard_map/while/body/eval_jaxpr/ppermute | solution.py:15
  389.2 19.1 %collective-permute-start = (f32[2560,128]{1,0:T(8,128)S(1)}, f32[2560,128]{1,0:T(8,128)S(1)}, u32[]{:S(2)}, u32[]{:S(2)}) collective-permute-start(f32[2560,128]{1,0:T(8,128)S(1)} %get-tuple-element.197), channel_id=1, source_target_pairs={{0,8},{8,16},{16,24},{24,32},{32,40},{40,48},{48,56},{56,64},{64,7... | collective-permute-start | bytes 3932168 | tf_op jit(solution)/shard_map/while/body/eval_jaxpr/ppermute | solution.py:15
  420.1 19.2 %collective-permute-start = (f32[2560,128]{1,0:T(8,128)S(1)}, f32[2560,128]{1,0:T(8,128)S(1)}, u32[]{:S(2)}, u32[]{:S(2)}) collective-permute-start(f32[2560,128]{1,0:T(8,128)S(1)} %get-tuple-element.197), channel_id=1, source_target_pairs={{0,8},{8,16},{16,24},{24,32},{32,40},{40,48},{48,56},{56,64},{64,7... | collective-permute-start | bytes 3932168 | tf_op jit(solution)/shard_map/while/body/eval_jaxpr/ppermute | solution.py:15
  451.0 19.1 %collective-permute-start = (f32[2560,128]{1,0:T(8,128)S(1)}, f32[2560,128]{1,0:T(8,128)S(1)}, u32[]{:S(2)}, u32[]{:S(2)}) collective-permute-start(f32[2560,128]{1,0:T(8,128)S(1)} %get-tuple-element.197), channel_id=1, source_target_pairs={{0,8},{8,16},{16,24},{24,32},{32,40},{40,48},{48,56},{56,64},{64,7... | collective-permute-start | bytes 3932168 | tf_op jit(solution)/shard_map/while/body/eval_jaxpr/ppermute | solution.py:15
  482.0 19.2 %collective-permute-start = (f32[2560,128]{1,0:T(8,128)S(1)}, f32[2560,128]{1,0:T(8,128)S(1)}, u32[]{:S(2)}, u32[]{:S(2)}) collective-permute-start(f32[2560,128]{1,0:T(8,128)S(1)} %get-tuple-element.197), channel_id=1, source_target_pairs={{0,8},{8,16},{16,24},{24,32},{32,40},{40,48},{48,56},{56,64},{64,7... | collective-permute-start | bytes 3932168 | tf_op jit(solution)/shard_map/while/body/eval_jaxpr/ppermute | solution.py:15
  512.9 493.6 %all-reduce.5.cloned.1.call-start = ((), (), s32[]{:S(2)}) async-start(), calls=%async_computation.1 | async-start | bytes 1048576 | tf_op jit(solution)/shard_map/psum | solution.py:56
Sparse Core Ops, SparseCore 0:
  513.0 358.0 all-reduce.2
  884.4 122.0 all-reduce.4
where the time goes:
time: 1020 us
  waiting for transfers between devices  731 us (72%)
  matrix products  205 us (20%)
  local copies, waits for them, and re-layouts  31.5 us (3%)
  starting transfers between devices  21.2 us (2%)
  between operations  13.5 us (1%)
  other arithmetic  12.6 us (1%)
    psum x1, waiting for transfers between devices, body(): summed = lax.psum(fitted, 'orb')  358 us
    ppermute x15, waiting for transfers between devices, shifted(): return lax.ppermute(value, axis, pairs)  251 us
    dot_general x16, matrix products, transform(): jnp.einsum('qml,li->qmi', masked_factors, panel, precision=lax.Precision....  192 us
    psum x1, waiting for transfers between devices, body(): kblock = lax.psum(partial_rows, 'aux')  122 us
    ppermute x15, starting transfers between devices, shifted(): return lax.ppermute(value, axis, pairs)  20.9 us
  transfers between devices with their start and end apart: 17, of which 17 were waited for; matrix products, arithmetic and copies ran while one was open for 0% of the time, Pallas kernels for 0%

commit v1 on v0

v1 whole, which is shorter than its diff:
```python
import functools
import math

import jax
import jax.numpy as jnp
from jax import lax
from jax.experimental import pallas as pl
from jax.experimental.pallas import tpu as pltpu
from jax.sharding import PartitionSpec as P

BLK = 128
NOCC = 2048
F32 = jnp.float32
BF16 = jnp.bfloat16
VMEM_LIMIT = 56 * 1024 * 1024
NT = (((1,), (1,)), ((), ()))


def aux_pairs(move):
    pairs = []
    for z in range(2):
        for x in range(4):
            for core in range(2):
                z2, x2, core2 = move(z, x, core)
                pairs.append((z * 8 + x * 2 + core, z2 * 8 + (x2 % 4) * 2 + core2))
    return pairs


def orb_pairs(move):
    pairs = []
    for y in range(4):
        for h in range(2):
            y2, h2 = move(y, h)
            pairs.append((y * 2 + h, (y2 % 4) * 2 + h2))
    return pairs


MOVES = {
    "x+": ("aux", aux_pairs(lambda z, x, c: (z, x + 1, c))),
    "x-": ("aux", aux_pairs(lambda z, x, c: (z, x - 1, c))),
    "xa": ("aux", aux_pairs(lambda z, x, c: (z, x ^ 1, c))),
    "xb": ("aux", aux_pairs(lambda z, x, c: (z, 3 - x, c))),
    "zl": ("aux", aux_pairs(lambda z, x, c: (1 - z, x, c))),
    "core": ("aux", aux_pairs(lambda z, x, c: (z, x, 1 - c))),
    "y+": ("orb", orb_pairs(lambda y, h: (y + 1, h))),
    "y-": ("orb", orb_pairs(lambda y, h: (y - 1, h))),
    "zh": ("orb", orb_pairs(lambda y, h: (y, 1 - h))),
}


def move(value, name):
    axis, pairs = MOVES[name]
    return lax.ppermute(value, axis, pairs)


def params():
    return pltpu.CompilerParams(vmem_limit_bytes=VMEM_LIMIT)


def whole(shape):
    return pl.BlockSpec(shape, lambda *_: tuple(0 for _ in shape))


SMEM = pl.BlockSpec(memory_space=pltpu.SMEM)

SEGMENTS = ((2, 0), (1, 1), (2, 1), (3, 0), (1, 0), (3, 1), (0, 0), (0, 1))
GROUPS = (2, 2, 1, 1, 2)


def transpose_panel(occupied, c_mask):
    depth, width = occupied.shape

    def kernel(mask_ref, c_ref, out_ref):
        for k in range(depth // BLK):
            keep = mask_ref[k, 0].astype(F32)
            out_ref[:, k * BLK : (k + 1) * BLK] = (c_ref[k * BLK : (k + 1) * BLK, :] * keep).T

    return pl.pallas_call(
        kernel,
        out_shape=jax.ShapeDtypeStruct((width, depth), F32),
        in_specs=[SMEM, whole(occupied.shape)],
        out_specs=whole((width, depth)),
        compiler_params=params(),
        name="panel",
    )(c_mask, occupied)


def split_factors(factors, mask):
    rows, depth = factors.shape

    def kernel(mask_ref, b_ref, hi_ref, lo_ref):
        row = pl.program_id(0)
        for k in range(depth // BLK):
            cols = slice(k * BLK, (k + 1) * BLK)
            value = b_ref[:, cols] * mask_ref[row, k]
            hi = value.astype(BF16)
            hi_ref[:, cols] = hi
            lo_ref[:, cols] = (value - hi.astype(F32)).astype(BF16)

    block = pl.BlockSpec((BLK, depth), lambda i: (i, 0))
    return pl.pallas_call(
        kernel,
        grid=(rows // BLK,),
        out_shape=[jax.ShapeDtypeStruct((rows, depth), BF16)] * 2,
        in_specs=[SMEM, block],
        out_specs=[block, block],
        compiler_params=params(),
        name="split",
    )(mask, factors)


def fitted_chunk(place, pieces, factors):
    own_hi, own_lo, other_hi, other_lo = factors
    rows, depth = own_hi.shape
    total = sum(piece.shape[0] for piece in pieces)
    seg = total // 8
    tile = 256
    steps = rows // tile
    count = len(pieces)

    def kernel(place_ref, *refs):
        piece_refs = refs[:count]
        own_hi_ref, own_lo_ref, other_hi_ref, other_lo_ref = refs[count : count + 4]
        out_refs = refs[count + 4 : count + 9]
        panel = refs[count + 9]
        step = pl.program_id(0)

        @pl.when(step == 0)
        def _():
            y, h = place_ref[0], place_ref[1]
            for index, (ahead, half) in enumerate(SEGMENTS):
                shard = lax.rem(y + ahead, 4)
                side = h if half == 0 else 1 - h
                parts = []
                for ref in piece_refs:
                    length = ref.shape[0] // 8
                    first = pl.multiple_of((shard * 2 + side) * length, length)
                    parts.append(ref[pl.ds(first, length), :])
                value = parts[0] if count == 1 else jnp.concatenate(parts, axis=0)
                hi = value.astype(BF16)
                panel[index * seg : (index + 1) * seg, :] = hi
                panel[total + index * seg : total + (index + 1) * seg, :] = (
                    value - hi.astype(F32)
                ).astype(BF16)

        def product(hi_ref, lo_ref):
            both = lax.dot_general(panel[...], hi_ref[...], NT, preferred_element_type=F32)
            rest = lax.dot_general(panel[:total, :], lo_ref[...], NT, preferred_element_type=F32)
            value = both[:total] + (both[total:] + rest)
            first = 0
            for ref, size in zip(out_refs, GROUPS):
                ref[...] = value[first * seg : (first + size) * seg, :]
                first += size

        @pl.when(step < steps)
        def _():
            product(own_hi_ref, own_lo_ref)

        @pl.when(step >= steps)
        def _():
            product(other_hi_ref, other_lo_ref)

    own_spec = pl.BlockSpec((tile, depth), lambda i: (jnp.minimum(i, steps - 1), 0))
    other_spec = pl.BlockSpec((tile, depth), lambda i: (jnp.maximum(i - steps, 0), 0))
    return pl.pallas_call(
        kernel,
        grid=(2 * steps,),
        out_shape=[jax.ShapeDtypeStruct((size * seg, 2 * rows), F32) for size in GROUPS],
        in_specs=[SMEM]
        + [whole(piece.shape) for piece in pieces]
        + [own_spec, own_spec, other_spec, other_spec],
        out_specs=[pl.BlockSpec((size * seg, tile), lambda i: (0, i)) for size in GROUPS],
        scratch_shapes=[pltpu.VMEM((2 * total, depth), BF16)],
        compiler_params=params(),
        cost_estimate=pl.CostEstimate(
            flops=6 * total * 2 * rows * depth, bytes_accessed=8 * rows * depth, transcendentals=0
        ),
        name="fitted",
    )(place, *pieces, own_hi, own_lo, other_hi, other_lo)


def exchange_partial(place, kept, arrived, scale):
    rows = sum(part.shape[0] for part in kept)
    width = kept[0].shape[1] // 2
    half_width = width // 2
    count = len(kept)

    def kernel(place_ref, *refs):
        kept_refs, arrived_refs = refs[:count], refs[count : 2 * count]
        send_ref = refs[2 * count]
        out_refs = refs[2 * count + 1 : 2 * count + 6]
        full, hi_ref, lo_ref = refs[2 * count + 6 :]
        y, h, core = place_ref[0], place_ref[1], place_ref[2]
        first = 0
        for kept_ref, arrived_ref in zip(kept_refs, arrived_refs):
            length = kept_ref.shape[0]
            value = kept_ref[...] + arrived_ref[...]
            full[first : first + length, :] = value[:, :width]
            full[rows + first : rows + first + length, :] = value[:, width:]
            first += length
        value = full[...]
        hi = value.astype(BF16)
        hi_ref[...] = hi
        lo_ref[...] = (value - hi.astype(F32)).astype(BF16)
        mine = pl.ds(pl.multiple_of(core * half_width, half_width), half_width)
        theirs = pl.ds(pl.multiple_of((1 - core) * half_width, half_width), half_width)

        def product(left, columns):
            left_hi = left.astype(BF16)
            left_lo = (left - left_hi.astype(F32)).astype(BF16)
            right_hi, right_lo = hi_ref[:, columns], lo_ref[:, columns]
            value = jnp.dot(left_hi, right_hi, preferred_element_type=F32)
            value += jnp.dot(left_hi, right_lo, preferred_element_type=F32)
            value += jnp.dot(left_lo, right_hi, preferred_element_type=F32)
            return value * scale

        index = 0
        for ref, size in zip(out_refs, GROUPS):
            for part in range(size):
                ahead, half = SEGMENTS[index]
                side = h if half == 0 else 1 - h
                block = lax.rem(y + ahead, 4) * 2 + side
                left = full[:, pl.ds(pl.multiple_of(block * BLK, BLK), BLK)].T
                ref[part * BLK : (part + 1) * BLK, :] = product(left, mine)
                send_ref[index * BLK : (index + 1) * BLK, :] = product(left, theirs)
                index += 1

    shapes = [(width, half_width)] + [(size * BLK, half_width) for size in GROUPS]
    return pl.pallas_call(
        kernel,
        out_shape=[jax.ShapeDtypeStruct(shape, F32) for shape in shapes],
        in_specs=[SMEM] + [whole(part.shape) for part in (*kept, *arrived)],
        out_specs=[whole(shape) for shape in shapes],
        scratch_shapes=[
            pltpu.VMEM((2 * rows, width), F32),
            pltpu.VMEM((2 * rows, width), BF16),
            pltpu.VMEM((2 * rows, width), BF16),
        ],
        compiler_params=params(),
        name="exchange",
    )(place, *kept, *arrived)


def scatter_y(parts):
    plus, minus, plus_late, minus_late, own = parts
    seg = plus_late.shape[0]
    from_below, from_above = move(plus, "y+"), move(minus, "y-")
    late_below = move(plus_late + from_below[:seg], "y+")
    late_above = move(minus_late + from_above[:seg], "y-")
    sent = own[seg:] + from_below[seg:] + late_above
    kept = own[:seg] + from_above[seg:] + late_below
    return kept, sent


def body(b_factors, occupied, b_mask, c_mask):
    aux, orb = lax.axis_index("aux"), lax.axis_index("orb")
    core = lax.rem(aux, 2)
    place = jnp.stack([lax.div(orb, 2), lax.rem(orb, 2), core]).astype(jnp.int32)
    naux = lax.axis_size("aux")
    factor = 1.0 / math.sqrt(b_factors.shape[0] * naux * NOCC)
    own_b, own_mask = b_factors[0], b_mask[0].astype(F32)

    panel = transpose_panel(occupied, c_mask)
    left, right, across = move(panel, "x+"), move(panel, "x-"), move(panel, "zl")
    other_b, other_mask = move(own_b, "core"), move(own_mask, "core")
    factors = (*split_factors(own_b, own_mask), *split_factors(other_b, other_mask))

    left2 = move(across, "x+")
    far = move(right, "x-")
    right2 = move(right, "zl")
    half = panel.shape[0] // 2
    far2 = (move(left2[:half], "x+"), move(right2[half:], "x-"))

    kept, arrived = [], []
    for pieces in ((panel,), (left, right, across), (left2, far, right2), far2):
        stay, sent = scatter_y(fitted_chunk(place, pieces, factors))
        kept.append(stay)
        arrived.append(move(sent, "zh"))

    send, *parts = exchange_partial(place, kept, arrived, factor)
    other = move(send, "core")
    first, summed = 0, []
    for part in parts:
        size = part.shape[0]
        summed.append(part + other[first : first + size])
        first += size
    stay, sent = scatter_y(summed)
    block = stay + move(sent, "zh")
    for name in ("zl", "xa", "xb"):
        block = block + move(block, name)
    other = move(block, "core")
    low = jnp.where(core == 0, block, other)
    high = jnp.where(core == 0, other, block)
    return jnp.concatenate([low, high], axis=1)


def solution(mesh):
    placed = (P("aux", None, "orb"), P("orb", "aux"), P("aux", None, "orb"), P("orb", "aux"))
    return jax.shard_map(
        body, mesh=mesh, in_specs=placed, out_specs=P("orb", None), check_vma=False
    )
```

time: 1020 us -> 311 us (0.30)
  waiting for transfers between devices: 731 us -> 131 us
  matrix products: 205 us -> 0 us
  Pallas kernels: 0 us -> 98.6 us
  starting transfers between devices: 21.2 us -> 66.7 us
  local copies, waits for them, and re-layouts: 31.5 us -> 4.9 us
  between operations: 13.5 us -> 0.39 us
    psum x2 -> x0, waiting for transfers between devices: 480 us -> none  [the longest x1 358 us: body(): summed = lax.psum(fitted, 'orb')]
    dot_general x17 -> x0, matrix products: 205 us -> none  [the longest x16 192 us: transform(): jnp.einsum('qml,li->qmi', masked_factors, panel, precision=lax.Precision....]
    ppermute x15 -> x40, waiting for transfers between devices: 251 us -> 131 us  [move(): return lax.ppermute(value, axis, pairs)]
    pallas_call x0 -> x8, Pallas kernels: none -> 98.6 us  [the longest x4 68.4 us: fitted_chunk(): pl.pallas_call(kernel, grid=(2 * steps,), out_shape=[jax.ShapeDtypeStruct...]
    ppermute x15 -> x40, starting transfers between devices: 20.9 us -> 66.7 us  [move(): return lax.ppermute(value, axis, pairs)]
    while x16 -> x0, local copies, waits for them, and re-layouts: 12.9 us -> none  [the longest x1 11.6 us: body(): unused, fitted = lax.fori_loop(1, naux_dev, advance, (panel_now, fitted))]
    unnamed x14 -> x53, local copies, waits for them, and re-layouts: 17.4 us -> 4.82 us
    mul x3 -> x0, other arithmetic: 12.6 us -> none  [the longest x1 10.3 us: body(): masked_factors = b_factors * expand(b_mask)]
  transfers between devices with their start and end apart: 17 -> 40, of which waited for: 17 -> 19; matrix products, arithmetic and copies ran while one was open for 0% -> 2% of each run, Pallas kernels for 0% -> 30%
where the time goes in v1:
time: 311 us; the launch traced here: 310 us
  waiting for transfers between devices  131 us (42%)
  Pallas kernels  98.6 us (32%)
  starting transfers between devices  66.7 us (21%)
  other arithmetic  8.95 us (3%)
  local copies, waits for them, and re-layouts  4.9 us (2%)
    ppermute x40, waiting for transfers between devices, move(): return lax.ppermute(value, axis, pairs)  131 us
    pallas_call x4, Pallas kernels, fitted_chunk(): pl.pallas_call(kernel, grid=(2 * steps,), out_shape=[jax.ShapeDtypeStruct...  68.4 us
    ppermute x40, starting transfers between devices, move(): return lax.ppermute(value, axis, pairs)  66.7 us
    pallas_call x2, Pallas kernels, split_factors(): pl.pallas_call(kernel, grid=(rows // BLK,), out_shape=[jax.ShapeDtypeStru...  21.8 us
  transfers between devices with their start and end apart: 40, of which 19 were waited for; matrix products, arithmetic and copies ran while one was open for 2% of the time, Pallas kernels for 30%

profile of v1, /device:TPU:1, one launch (start us, length us, event | category | flops | bytes accessed | tf_op | source)
XLA Modules:
  0.0 310.1 jit_solution(3016613580412302589)
XLA Ops:
  0.0 1.4 collective-permute-start.1
  1.4 1.3 copy.5.mask_ref
  2.8 2.8 panel.1.refs_0_
  5.6 2.6 collective-permute-start.6
  8.1 1.6 collective-permute-start.7
  9.8 26.9 %collective-permute-done.6.refs_1_ = f32[128,2560]{1,0:T(8,128)} collective-permute-done((f32[128,2560]{1,0:T(8,128)}, f32[128,2560]{1,0:T(8,128)}, u32[]{:S(2)}, u32[]{:S(2)}) %collective-permute-start.6) | collective-permute-done | bytes 1310752 | tf_op jit(solution)/shard_map/ppermute | solution.py:53
  36.7 1.6 collective-permute-start.13
  38.3 0.6 collective-permute-done.7.refs_2_
  39.2 2.6 collective-permute-start.12
  41.8 25.1 %collective-permute-done.13.refs_2_ = f32[128,2560]{1,0:T(8,128)S(1)} collective-permute-done((f32[128,2560]{1,0:T(8,128)}, f32[128,2560]{1,0:T(8,128)S(1)}, u32[]{:S(2)}, u32[]{:S(2)}) %collective-permute-start.13) | collective-permute-done | bytes 1310752 | tf_op jit(solution)/shard_map/ppermute | solution.py:53
  66.9 3.5 %collective-permute-start.18 = (f32[64,2560]{1,0:T(8,128)S(1)}, f32[64,2560]{1,0:T(8,128)S(1)}, u32[]{:S(2)}, u32[]{:S(2)}) collective-permute-start(f32[64,2560]{1,0:T(8,128)S(1)} %slice.155), channel_id=1, source_target_pairs={{0,48},{8,56},{16,0},{24,8},{32,16},{40,24},{48,32},{56,40},{64,11... | collective-permute-start | bytes 1966088 | tf_op jit(solution)/shard_map/ppermute | solution.py:53
  70.6 0.9 copy-done.12
  71.5 1.6 collective-permute-start
  73.2 0.6 pad_add_fusion.place_ref
  73.8 10.9 %split.2 = (bf16[1024,2560]{1,0:T(8,128)(2,1)}, bf16[1024,2560]{1,0:T(8,128)(2,1)}) custom-call(f32[8,20]{1,0:T(8,128)} %copy-done.21, f32[1024,2560]{1,0:T(8,128)} %bitcast.7), custom_call_target="tpu_custom_call" | custom-call | tf_op jit(solution)/shard_map/split/pallas_call | solution.py:101
  85.4 10.8 %split.3 = (bf16[1024,2560]{1,0:T(8,128)(2,1)}, bf16[1024,2560]{1,0:T(8,128)(2,1)}) custom-call(f32[8,20]{1,0:T(8,128)} %copy-done.22, f32[1024,2560]{1,0:T(8,128)} %collective-permute-done.1.b_ref), custom_call_target="tpu_custom_call" | custom-call | tf_op jit(solution)/shard_map/split/pallas_call | solution.py:101
  96.2 0.8 copy-done.3
  97.3 14.2 %fitted.7 = (f32[32,2048]{1,0:T(8,128)}, f32[32,2048]{1,0:T(8,128)}, f32[16,2048]{1,0:T(8,128)}, f32[16,2048]{1,0:T(8,128)}, f32[32,2048]{1,0:T(8,128)}) custom-call(s32[3]{0:T(128)} %pad_add_fusion.place_ref, f32[64,2560]{1,0:T(8,128)} %copy-done.4, f32[64,2560]{1,0:T(8,128)} %copy-done.3, bf16[1024,2560]{1,0:T(8,128)(2,1)} %get-tuple-element.35.refs_1_.refs_3_.refs_2_, ...), custom_call_target="tpu_custom_call" | custom-call | flops 4026531840 | bytes 20971520 | tf_op jit(solution)/shard_map/fitted/pallas_call | solution.py:165
  111.4 1.3 collective-permute-start.20
  112.8 1.5 collective-permute-start.19
  114.3 20.0 %fitted.6 = (f32[96,2048]{1,0:T(8,128)}, f32[96,2048]{1,0:T(8,128)}, f32[48,2048]{1,0:T(8,128)}, f32[48,2048]{1,0:T(8,128)}, f32[96,2048]{1,0:T(8,128)}) custom-call(s32[3]{0:T(128)} %pad_add_fusion.place_ref, f32[128,2560]{1,0:T(8,128)} %copy-done.12, f32[128,2560]{1,0:T(8,128)} %collective-permute-done.12.refs_1_, f32[128,2560]{1,0:T(8,128)} %copy-done.11, ...), custom_call_target="tpu_custom_call" | custom-call | flops 12079595520 | bytes 20971520 | tf_op jit(solution)/shard_map/fitted/pallas_call | solution.py:165
  134.4 2.7 collective-permute-start.14
  137.0 20.0 %fitted.5 = (f32[96,2048]{1,0:T(8,128)}, f32[96,2048]{1,0:T(8,128)}, f32[48,2048]{1,0:T(8,128)}, f32[48,2048]{1,0:T(8,128)}, f32[96,2048]{1,0:T(8,128)}) custom-call(s32[3]{0:T(128)} %pad_add_fusion.place_ref, f32[128,2560]{1,0:T(8,128)} %collective-permute-done.5.refs_0_, f32[128,2560]{1,0:T(8,128)} %collective-permute-done.6.refs_1_, ...), custom_call_target="tpu_custom_call" | custom-call | flops 12079595520 | bytes 20971520 | tf_op jit(solution)/shard_map/fitted/pallas_call | solution.py:165
  157.1 14.3 %fitted.4 = (f32[32,2048]{1,0:T(8,128)}, f32[32,2048]{1,0:T(8,128)}, f32[16,2048]{1,0:T(8,128)}, f32[16,2048]{1,0:T(8,128)}, f32[32,2048]{1,0:T(8,128)}) custom-call(s32[3]{0:T(128)} %pad_add_fusion.place_ref, f32[128,2560]{1,0:T(8,128)} %panel.1.refs_0_, bf16[1024,2560]{1,0:T(8,128)(2,1)} %get-tuple-element.35.refs_1_.refs_3_.refs_2_, ...), custom_call_target="tpu_custom_call" | custom-call | flops 4026531840 | bytes 20971520 | tf_op jit(solution)/shard_map/fitted/pallas_call | solution.py:165
  171.6 2.7 collective-permute-start.2
  174.3 7.9 %collective-permute-done.3 = f32[32,2048]{1,0:T(8,128)S(1)} collective-permute-done((f32[32,2048]{1,0:T(8,128)}, f32[32,2048]{1,0:T(8,128)S(1)}, u32[]{:S(2)}, u32[]{:S(2)}) %collective-permute-start.3) | collective-permute-done | bytes 262176 | tf_op jit(solution)/shard_map/ppermute | solution.py:53
  182.2 1.0 slice_add_fusion.23
  183.2 2.7 collective-permute-start.28
  185.9 0.9 slice_add_fusion.19
  187.2 0.6 collective-permute-done.28
  187.9 0.8 collective-permute-start.4
  188.7 0.7 fusion.7
  189.4 2.3 collective-permute-start.22
  191.7 3.5 %collective-permute-start.29 = (f32[16,2048]{1,0:T(8,128)S(1)}, f32[16,2048]{1,0:T(8,128)S(1)}, u32[]{:S(2)}, u32[]{:S(2)}) collective-permute-start(f32[16,2048]{1,0:T(8,128)S(1)} %get-tuple-element.76), channel_id=1, source_target_pairs={{0,1},{1,0},{2,3},{3,2},{4,5},{5,4},{6,7},{7,6},{8,9},{9,8},{10,11... | collective-permute-start | bytes 393224 | tf_op jit(solution)/shard_map/ppermute | solution.py:53
  195.4 8.0 %collective-permute-done.8 = f32[96,2048]{1,0:T(8,128)S(1)} collective-permute-done((f32[96,2048]{1,0:T(8,128)S(1)}, f32[96,2048]{1,0:T(8,128)S(1)}, u32[]{:S(2)}, u32[]{:S(2)}) %collective-permute-start.8) | collective-permute-done | bytes 786464 | tf_op jit(solution)/shard_map/ppermute | solution.py:53
  203.4 3.4 %collective-permute-start.26 = (f32[48,2048]{1,0:T(8,128)S(1)}, f32[48,2048]{1,0:T(8,128)S(1)}, u32[]{:S(2)}, u32[]{:S(2)}) collective-permute-start(f32[48,2048]{1,0:T(8,128)S(1)} %slice_add_fusion.3), channel_id=1, source_target_pairs={{0,6},{1,7},{2,0},{3,1},{4,2},{5,3},{6,4},{7,5},{8,14},{9,15},{10,... | collective-permute-start | bytes 1179656 | tf_op jit(solution)/shard_map/ppermute | solution.py:53
  206.9 6.8 %collective-permute-done.26 = f32[48,2048]{1,0:T(8,128)S(1)} collective-permute-done((f32[48,2048]{1,0:T(8,128)S(1)}, f32[48,2048]{1,0:T(8,128)S(1)}, u32[]{:S(2)}, u32[]{:S(2)}) %collective-permute-start.26) | collective-permute-done | bytes 393248 | tf_op jit(solution)/shard_map/ppermute | solution.py:53
  213.8 3.4 %collective-permute-start.24 = (f32[48,2048]{1,0:T(8,128)S(1)}, f32[48,2048]{1,0:T(8,128)S(1)}, u32[]{:S(2)}, u32[]{:S(2)}) collective-permute-start(f32[48,2048]{1,0:T(8,128)S(1)} %slice_add_fusion.5), channel_id=1, source_target_pairs={{0,6},{1,7},{2,0},{3,1},{4,2},{5,3},{6,4},{7,5},{8,14},{9,15},{10,... | collective-permute-start | bytes 1179656 | tf_op jit(solution)/shard_map/ppermute | solution.py:53
  217.2 0.9 fusion
  218.1 3.4 %collective-permute-start.27 = (f32[48,2048]{1,0:T(8,128)S(1)}, f32[48,2048]{1,0:T(8,128)S(1)}, u32[]{:S(2)}, u32[]{:S(2)}) collective-permute-start(f32[48,2048]{1,0:T(8,128)S(1)} %get-tuple-element.70), channel_id=1, source_target_pairs={{0,1},{1,0},{2,3},{3,2},{4,5},{5,4},{6,7},{7,6},{8,9},{9,8},{10,11... | collective-permute-start | bytes 1179656 | tf_op jit(solution)/shard_map/ppermute | solution.py:53
  221.9 0.9 fusion.1
  222.8 3.4 %collective-permute-start.25 = (f32[48,2048]{1,0:T(8,128)S(1)}, f32[48,2048]{1,0:T(8,128)S(1)}, u32[]{:S(2)}, u32[]{:S(2)}) collective-permute-start(f32[48,2048]{1,0:T(8,128)S(1)} %get-tuple-element.72), channel_id=1, source_target_pairs={{0,1},{1,0},{2,3},{3,2},{4,5},{5,4},{6,7},{7,6},{8,9},{9,8},{10,11... | collective-permute-start | bytes 1179656 | tf_op jit(solution)/shard_map/ppermute | solution.py:53
  226.2 0.7 fusion.8
  227.0 11.7 %collective-permute-done.23.refs_4_ = f32[16,2048]{1,0:T(8,128)S(1)} collective-permute-done((f32[16,2048]{1,0:T(8,128)S(1)}, f32[16,2048]{1,0:T(8,128)S(1)}, u32[]{:S(2)}, u32[]{:S(2)}) %collective-permute-start.23) | collective-permute-done | bytes 131104 | tf_op jit(solution)/shard_map/ppermute | solution.py:53
  238.7 0.6 copy-done.20
  239.6 5.5 %exchange.1 = (f32[1024,512]{1,0:T(8,128)}, f32[256,512]{1,0:T(8,128)}, f32[256,512]{1,0:T(8,128)}, f32[128,512]{1,0:T(8,128)}, f32[128,512]{1,0:T(8,128)}, /*index=5*/f32[256,512]{1,0:T(8,128)}) custom-call(s32[3]{0:T(128)} %pad_add_fusion.place_ref, f32[16,2048]{1,0:T(8,128)} %get-tuple-element.79.refs_0_, f32[48,2048]{1,0:T(8,128)} %get-tuple-element.73.refs_1_, ...), custom_call_target="tpu_custom_call" | custom-call | tf_op jit(solution)/shard_map/exchange/pallas_call | solution.py:229
  245.1 4.4 %collective-permute-start.30 = (f32[1024,512]{1,0:T(8,128)}, f32[1024,512]{1,0:T(8,128)S(1)}, u32[]{:S(2)}, u32[]{:S(2)}) collective-permute-start(f32[1024,512]{1,0:T(8,128)} %get-tuple-element.60), channel_id=1, source_target_pairs={{0,8},{8,0},{16,24},{24,16},{32,40},{40,32},{48,56},{56,48},{64,72... | collective-permute-start | bytes 6291464 | tf_op jit(solution)/shard_map/ppermute | solution.py:53
  249.5 4.0 %collective-permute-done.30 = f32[1024,512]{1,0:T(8,128)S(1)} collective-permute-done((f32[1024,512]{1,0:T(8,128)}, f32[1024,512]{1,0:T(8,128)S(1)}, u32[]{:S(2)}, u32[]{:S(2)}) %collective-permute-start.30) | collective-permute-done | bytes 2097184 | tf_op jit(solution)/shard_map/ppermute | solution.py:53
  253.5 1.8 slice_add_fusion.2
  255.3 1.5 collective-permute-start.32
  256.8 11.7 %collective-permute-done.31 = f32[256,512]{1,0:T(8,128)S(1)} collective-permute-done((f32[256,512]{1,0:T(8,128)S(1)}, f32[256,512]{1,0:T(8,128)S(1)}, u32[]{:S(2)}, u32[]{:S(2)}) %collective-permute-start.31) | collective-permute-done | bytes 524320 | tf_op jit(solution)/shard_map/ppermute | solution.py:53
  268.4 1.3 collective-permute-done.32
  270.2 1.3 collective-permute-start.33
  271.4 5.1 %collective-permute-done.34 = f32[128,512]{1,0:T(8,128)S(1)} collective-permute-done((f32[128,512]{1,0:T(8,128)S(1)}, f32[128,512]{1,0:T(8,128)S(1)}, u32[]{:S(2)}, u32[]{:S(2)}) %collective-permute-start.34) | collective-permute-done | bytes 262176 | tf_op jit(solution)/shard_map/ppermute | solution.py:53
  276.6 3.3 %collective-permute-start.35 = (f32[128,512]{1,0:T(8,128)S(1)}, f32[128,512]{1,0:T(8,128)S(1)}, u32[]{:S(2)}, u32[]{:S(2)}) collective-permute-start(f32[128,512]{1,0:T(8,128)S(1)} %fusion.4), channel_id=1, source_target_pairs={{0,1},{1,0},{2,3},{3,2},{4,5},{5,4},{6,7},{7,6},{8,9},{9,8},{10,11... | collective-permute-start | bytes 786440 | tf_op jit(solution)/shard_map/ppermute | solution.py:53
  280.0 4.5 %collective-permute-done.35 = f32[128,512]{1,0:T(8,128)S(1)} collective-permute-done((f32[128,512]{1,0:T(8,128)S(1)}, f32[128,512]{1,0:T(8,128)S(1)}, u32[]{:S(2)}, u32[]{:S(2)}) %collective-permute-start.35) | collective-permute-done | bytes 262176 | tf_op jit(solution)/shard_map/ppermute | solution.py:53
  284.6 0.8 collective-permute-start.36
  285.4 4.7 %collective-permute-done.36 = f32[128,512]{1,0:T(8,128)S(1)} collective-permute-done((f32[128,512]{1,0:T(8,128)S(1)}, f32[128,512]{1,0:T(8,128)S(1)}, u32[]{:S(2)}, u32[]{:S(2)}) %collective-permute-start.36) | collective-permute-done | bytes 262176 | tf_op jit(solution)/shard_map/ppermute | solution.py:53
  290.2 5.2 %collective-permute-done.37 = f32[128,512]{1,0:T(8,128)S(1)} collective-permute-done((f32[128,512]{1,0:T(8,128)S(1)}, f32[128,512]{1,0:T(8,128)S(1)}, u32[]{:S(2)}, u32[]{:S(2)}) %collective-permute-start.37) | collective-permute-done | bytes 262176 | tf_op jit(solution)/shard_map/ppermute | solution.py:53
  295.5 2.0 collective-permute-start.38
  297.5 4.5 %collective-permute-done.38 = f32[128,512]{1,0:T(8,128)S(1)} collective-permute-done((f32[128,512]{1,0:T(8,128)S(1)}, f32[128,512]{1,0:T(8,128)S(1)}, u32[]{:S(2)}, u32[]{:S(2)}) %collective-permute-start.38) | collective-permute-done | bytes 262176 | tf_op jit(solution)/shard_map/ppermute | solution.py:53
  302.0 6.1 %collective-permute-start.39 = (f32[128,512]{1,0:T(8,128)S(1)}, f32[128,512]{1,0:T(8,128)S(1)}, u32[]{:S(2)}, u32[]{:S(2)}) collective-permute-start(f32[128,512]{1,0:T(8,128)S(1)} %add.155), channel_id=1, source_target_pairs={{0,8},{8,0},{16,24},{24,16},{32,40},{40,32},{48,56},{56,48},{64,72... | collective-permute-start | bytes 786440 | tf_op jit(solution)/shard_map/ppermute | solution.py:53
  308.1 1.2 collective-permute-done.39
  309.3 0.8 pad_maximum_fusion
  (102 shorter events, 4.1 us)
Async XLA Ops:
  0.0 84.9 %collective-permute-start.1 = (f32[1024,2560]{1,0:T(8,128)}, f32[1024,2560]{1,0:T(8,128)}, u32[]{:S(2)}, u32[]{:S(2)}) collective-permute-start(f32[1024,2560]{1,0:T(8,128)} %bitcast.6), channel_id=1, source_target_pairs={{0,8},{8,0},{16,24},{24,16},{32,40},{40,32},{48,56},{56,48},{64,72... | collective-permute-start | bytes 31457288 | tf_op jit(solution)/shard_map/ppermute | solution.py:53
  2.8 67.8 %copy-start.23 = (s32[1,8,20]{2,1,0:T(8,128)S(1)}, s32[1,8,20]{2,1,0:T(8,128)}, u32[]{:S(2)}) copy-start(s32[1,8,20]{2,1,0:T(8,128)} %param.6) | copy-start | bytes 1924
  5.6 31.1 %collective-permute-start.6 = (f32[128,2560]{1,0:T(8,128)}, f32[128,2560]{1,0:T(8,128)}, u32[]{:S(2)}, u32[]{:S(2)}) collective-permute-start(f32[128,2560]{1,0:T(8,128)} %panel.1.refs_0_), channel_id=1, source_target_pairs={{0,48},{8,56},{16,0},{24,8},{32,16},{40,24},{48,32},{56,40},{64,11... | collective-permute-start | bytes 3932168 | tf_op jit(solution)/shard_map/ppermute | solution.py:53
  8.1 30.7 %collective-permute-start.7 = (f32[128,2560]{1,0:T(8,128)}, f32[128,2560]{1,0:T(8,128)S(1)}, u32[]{:S(2)}, u32[]{:S(2)}) collective-permute-start(f32[128,2560]{1,0:T(8,128)} %panel.1.refs_0_), channel_id=1, source_target_pairs={{0,64},{8,72},{16,80},{24,88},{32,96},{40,104},{48,112},{56,120},{... | collective-permute-start | bytes 3932168 | tf_op jit(solution)/shard_map/ppermute | solution.py:53
  36.7 30.2 %collective-permute-start.13 = (f32[128,2560]{1,0:T(8,128)}, f32[128,2560]{1,0:T(8,128)S(1)}, u32[]{:S(2)}, u32[]{:S(2)}) collective-permute-start(f32[128,2560]{1,0:T(8,128)} %collective-permute-done.6.refs_1_), channel_id=1, source_target_pairs={{0,64},{8,72},{16,80},{24,88},{32,96},{40,104},{48,112},{56,120},{... | collective-permute-start | bytes 3932168 | tf_op jit(solution)/shard_map/ppermute | solution.py:53
  38.9 34.3 %copy-start.24 = (f32[128,2560]{1,0:T(8,128)}, f32[128,2560]{1,0:T(8,128)S(1)}, u32[]{:S(2)}) copy-start(f32[128,2560]{1,0:T(8,128)S(1)} %collective-permute-done.7.refs_2_) | copy-start | bytes 3932164
  38.9 31.5 %collective-permute-start.11 = (f32[128,2560]{1,0:T(8,128)S(1)}, f32[128,2560]{1,0:T(8,128)S(1)}, u32[]{:S(2)}, u32[]{:S(2)}) collective-permute-start(f32[128,2560]{1,0:T(8,128)S(1)} %collective-permute-done.7.refs_2_), channel_id=1, source_target_pairs={{0,16},{8,24},{16,32},{24,40},{32,48},{40,56},{48,0},{56,8},{64,80... | collective-permute-start | bytes 3932168 | tf_op jit(solution)/shard_map/ppermute | solution.py:53
  39.2 75.1 %collective-permute-start.12 = (f32[128,2560]{1,0:T(8,128)}, f32[128,2560]{1,0:T(8,128)}, u32[]{:S(2)}, u32[]{:S(2)}) collective-permute-start(f32[128,2560]{1,0:T(8,128)} %collective-permute-done.6.refs_1_), channel_id=1, source_target_pairs={{0,48},{8,56},{16,0},{24,8},{32,16},{40,24},{48,32},{56,40},{64,11... | collective-permute-start | bytes 3932168 | tf_op jit(solution)/shard_map/ppermute | solution.py:53
  66.9 3.7 %copy-start.11 = (f32[128,2560]{1,0:T(8,128)}, f32[128,2560]{1,0:T(8,128)S(1)}, u32[]{:S(2)}) copy-start(f32[128,2560]{1,0:T(8,128)S(1)} %collective-permute-done.13.refs_2_) | copy-start | bytes 3932164
  66.9 29.3 %collective-permute-start.18 = (f32[64,2560]{1,0:T(8,128)S(1)}, f32[64,2560]{1,0:T(8,128)S(1)}, u32[]{:S(2)}, u32[]{:S(2)}) collective-permute-start(f32[64,2560]{1,0:T(8,128)S(1)} %slice.155), channel_id=1, source_target_pairs={{0,48},{8,56},{16,0},{24,8},{32,16},{40,24},{48,32},{56,40},{64,11... | collective-permute-start | bytes 1966088 | tf_op jit(solution)/shard_map/ppermute | solution.py:53
  70.4 1.1 copy-start.12
  70.5 25.7 %collective-permute-start.17 = (f32[64,2560]{1,0:T(8,128)S(1)}, f32[64,2560]{1,0:T(8,128)S(1)}, u32[]{:S(2)}, u32[]{:S(2)}) collective-permute-start(f32[64,2560]{1,0:T(8,128)S(1)} %slice.154), channel_id=1, source_target_pairs={{0,16},{8,24},{16,32},{24,40},{32,48},{40,56},{48,0},{56,8},{64,80... | collective-permute-start | bytes 1966088 | tf_op jit(solution)/shard_map/ppermute | solution.py:53
  71.5 2.3 copy-start.21
  71.5 13.2 %collective-permute-start = (f32[8,20]{1,0:T(8,128)S(1)}, f32[8,20]{1,0:T(8,128)S(1)}, u32[]{:S(2)}, u32[]{:S(2)}) collective-permute-start(f32[8,20]{1,0:T(8,128)S(1)} %convert_bitcast_fusion.mask_ref), channel_id=1, source_target_pairs={{0,8},{8,0},{16,24},{24,16},{32,40},{40,32},{48,56},{56,48},{64,72... | collective-permute-start | bytes 1928 | tf_op jit(solution)/shard_map/ppermute | solution.py:53
  73.8 10.9 %copy-start = (f32[128,2560]{1,0:T(8,128)S(1)}, f32[128,2560]{1,0:T(8,128)}, u32[]{:S(2)}) copy-start(f32[128,2560]{1,0:T(8,128)} %panel.1.refs_0_) | copy-start | bytes 3932164
  84.8 52.3 %collective-permute-start.5 = (f32[128,2560]{1,0:T(8,128)S(1)}, f32[128,2560]{1,0:T(8,128)}, u32[]{:S(2)}, u32[]{:S(2)}) collective-permute-start(f32[128,2560]{1,0:T(8,128)S(1)} %copy-done), channel_id=1, source_target_pairs={{0,16},{8,24},{16,32},{24,40},{32,48},{40,56},{48,0},{56,8},{64,80... | collective-permute-start | bytes 3932168 | tf_op jit(solution)/shard_map/ppermute | solution.py:53
  96.2 0.8 copy-start.3
  96.2 1.1 copy-start.4
  111.4 60.0 %collective-permute-start.20 = (f32[32,2048]{1,0:T(8,128)}, f32[32,2048]{1,0:T(8,128)S(1)}, u32[]{:S(2)}, u32[]{:S(2)}) collective-permute-start(f32[32,2048]{1,0:T(8,128)} %get-tuple-element.54), channel_id=1, source_target_pairs={{0,2},{1,3},{2,4},{3,5},{4,6},{5,7},{6,0},{7,1},{8,10},{9,11},{10,... | collective-permute-start | bytes 786440 | tf_op jit(solution)/shard_map/ppermute | solution.py:53
  112.8 58.8 %collective-permute-start.19 = (f32[32,2048]{1,0:T(8,128)}, f32[32,2048]{1,0:T(8,128)S(1)}, u32[]{:S(2)}, u32[]{:S(2)}) collective-permute-start(f32[32,2048]{1,0:T(8,128)} %get-tuple-element.52), channel_id=1, source_target_pairs={{0,6},{1,7},{2,0},{3,1},{4,2},{5,3},{6,4},{7,5},{8,14},{9,15},{10,... | collective-permute-start | bytes 786440 | tf_op jit(solution)/shard_map/ppermute | solution.py:53
  134.3 55.1 %collective-permute-start.15 = (f32[96,2048]{1,0:T(8,128)}, f32[96,2048]{1,0:T(8,128)S(1)}, u32[]{:S(2)}, u32[]{:S(2)}) collective-permute-start(f32[96,2048]{1,0:T(8,128)} %get-tuple-element.50), channel_id=1, source_target_pairs={{0,2},{1,3},{2,4},{3,5},{4,6},{5,7},{6,0},{7,1},{8,10},{9,11},{10,... | collective-permute-start | bytes 2359304 | tf_op jit(solution)/shard_map/ppermute | solution.py:53
  134.4 57.4 %collective-permute-start.14 = (f32[96,2048]{1,0:T(8,128)}, f32[96,2048]{1,0:T(8,128)S(1)}, u32[]{:S(2)}, u32[]{:S(2)}) collective-permute-start(f32[96,2048]{1,0:T(8,128)} %get-tuple-element.48), channel_id=1, source_target_pairs={{0,6},{1,7},{2,0},{3,1},{4,2},{5,3},{6,4},{7,5},{8,14},{9,15},{10,... | collective-permute-start | bytes 2359304 | tf_op jit(solution)/shard_map/ppermute | solution.py:53
  157.0 14.6 %copy-start.19 = (f32[16,2048]{1,0:T(8,128)S(1)}, f32[16,2048]{1,0:T(8,128)}, u32[]{:S(2)}) copy-start(f32[16,2048]{1,0:T(8,128)} %get-tuple-element.53) | copy-start | bytes 393220
  157.0 17.3 %copy-start.18 = (f32[16,2048]{1,0:T(8,128)S(1)}, f32[16,2048]{1,0:T(8,128)}, u32[]{:S(2)}) copy-start(f32[16,2048]{1,0:T(8,128)} %get-tuple-element.58) | copy-start | bytes 393220
  157.0 30.2 %copy-start.25 = (f32[96,2048]{1,0:T(8,128)S(1)}, f32[96,2048]{1,0:T(8,128)}, u32[]{:S(2)}) copy-start(f32[96,2048]{1,0:T(8,128)} %get-tuple-element.44) | copy-start | bytes 2359300
  157.0 31.7 %copy-start.14 = (f32[32,2048]{1,0:T(8,128)S(1)}, f32[32,2048]{1,0:T(8,128)}, u32[]{:S(2)}) copy-start(f32[32,2048]{1,0:T(8,128)} %get-tuple-element.51) | copy-start | bytes 786436
  157.0 38.2 %collective-permute-start.9 = (f32[96,2048]{1,0:T(8,128)}, f32[96,2048]{1,0:T(8,128)S(1)}, u32[]{:S(2)}, u32[]{:S(2)}) collective-permute-start(f32[96,2048]{1,0:T(8,128)} %get-tuple-element.46), channel_id=1, source_target_pairs={{0,2},{1,3},{2,4},{3,5},{4,6},{5,7},{6,0},{7,1},{8,10},{9,11},{10,... | collective-permute-start | bytes 2359304 | tf_op jit(solution)/shard_map/ppermute | solution.py:53
  171.4 20.2 %copy-start.9 = (f32[48,2048]{1,0:T(8,128)S(1)}, f32[48,2048]{1,0:T(8,128)}, u32[]{:S(2)}) copy-start(f32[48,2048]{1,0:T(8,128)} %get-tuple-element.49) | copy-start | bytes 1179652
  171.5 23.7 %copy-start.7 = (f32[48,2048]{1,0:T(8,128)S(1)}, f32[48,2048]{1,0:T(8,128)}, u32[]{:S(2)}) copy-start(f32[48,2048]{1,0:T(8,128)} %get-tuple-element.57) | copy-start | bytes 1179652
  171.5 10.7 %collective-permute-start.3 = (f32[32,2048]{1,0:T(8,128)}, f32[32,2048]{1,0:T(8,128)S(1)}, u32[]{:S(2)}, u32[]{:S(2)}) collective-permute-start(f32[32,2048]{1,0:T(8,128)} %get-tuple-element.42), channel_id=1, source_target_pairs={{0,2},{1,3},{2,4},{3,5},{4,6},{5,7},{6,0},{7,1},{8,10},{9,11},{10,... | collective-permute-start | bytes 786440 | tf_op jit(solution)/shard_map/ppermute | solution.py:53
  171.6 11.6 %collective-permute-start.2 = (f32[32,2048]{1,0:T(8,128)}, f32[32,2048]{1,0:T(8,128)S(1)}, u32[]{:S(2)}, u32[]{:S(2)}) collective-permute-start(f32[32,2048]{1,0:T(8,128)} %get-tuple-element.40), channel_id=1, source_target_pairs={{0,6},{1,7},{2,0},{3,1},{4,2},{5,3},{6,4},{7,5},{8,14},{9,15},{10,... | collective-permute-start | bytes 786440 | tf_op jit(solution)/shard_map/ppermute | solution.py:53
  182.2 5.0 %collective-permute-start.21 = (f32[16,2048]{1,0:T(8,128)S(1)}, f32[16,2048]{1,0:T(8,128)S(1)}, u32[]{:S(2)}, u32[]{:S(2)}) collective-permute-start(f32[16,2048]{1,0:T(8,128)S(1)} %slice_add_fusion.21), channel_id=1, source_target_pairs={{0,2},{1,3},{2,4},{3,5},{4,6},{5,7},{6,0},{7,1},{8,10},{9,11},{10,... | collective-permute-start | bytes 393224 | tf_op jit(solution)/shard_map/ppermute | solution.py:53
  182.2 13.1 %copy-start.10 = (f32[48,2048]{1,0:T(8,128)S(1)}, f32[48,2048]{1,0:T(8,128)}, u32[]{:S(2)}) copy-start(f32[48,2048]{1,0:T(8,128)} %get-tuple-element.45) | copy-start | bytes 1179652
  183.2 4.7 %collective-permute-start.28 = (f32[16,2048]{1,0:T(8,128)S(1)}, f32[16,2048]{1,0:T(8,128)S(1)}, u32[]{:S(2)}, u32[]{:S(2)}) collective-permute-start(f32[16,2048]{1,0:T(8,128)S(1)} %slice_add_fusion.17), channel_id=1, source_target_pairs={{0,6},{1,7},{2,0},{3,1},{4,2},{5,3},{6,4},{7,5},{8,14},{9,15},{10,... | collective-permute-start | bytes 393224 | tf_op jit(solution)/shard_map/ppermute | solution.py:53
  187.2 16.2 %collective-permute-start.8 = (f32[96,2048]{1,0:T(8,128)S(1)}, f32[96,2048]{1,0:T(8,128)S(1)}, u32[]{:S(2)}, u32[]{:S(2)}) collective-permute-start(f32[96,2048]{1,0:T(8,128)S(1)} %copy-done.25), channel_id=1, source_target_pairs={{0,6},{1,7},{2,0},{3,1},{4,2},{5,3},{6,4},{7,5},{8,14},{9,15},{10,... | collective-permute-start | bytes 2359304 | tf_op jit(solution)/shard_map/ppermute | solution.py:53
  187.9 38.4 %collective-permute-start.4 = (f32[16,2048]{1,0:T(8,128)S(1)}, f32[16,2048]{1,0:T(8,128)S(1)}, u32[]{:S(2)}, u32[]{:S(2)}) collective-permute-start(f32[16,2048]{1,0:T(8,128)S(1)} %slice_add_fusion.23), channel_id=1, source_target_pairs={{0,2},{1,3},{2,4},{3,5},{4,6},{5,7},{6,0},{7,1},{8,10},{9,11},{10,... | collective-permute-start | bytes 393224 | tf_op jit(solution)/shard_map/ppermute | solution.py:53
  188.7 18.1 %copy-start.8 = (f32[48,2048]{1,0:T(8,128)S(1)}, f32[48,2048]{1,0:T(8,128)}, u32[]{:S(2)}) copy-start(f32[48,2048]{1,0:T(8,128)} %get-tuple-element.56) | copy-start | bytes 1179652
  189.4 36.8 %collective-permute-start.22 = (f32[16,2048]{1,0:T(8,128)S(1)}, f32[16,2048]{1,0:T(8,128)S(1)}, u32[]{:S(2)}, u32[]{:S(2)}) collective-permute-start(f32[16,2048]{1,0:T(8,128)S(1)} %slice_add_fusion.19), channel_id=1, source_target_pairs={{0,6},{1,7},{2,0},{3,1},{4,2},{5,3},{6,4},{7,5},{8,14},{9,15},{10,... | collective-permute-start | bytes 393224 | tf_op jit(solution)/shard_map/ppermute | solution.py:53
  191.7 25.5 %copy-start.2 = (f32[96,2048]{1,0:T(8,128)S(1)}, f32[96,2048]{1,0:T(8,128)}, u32[]{:S(2)}) copy-start(f32[96,2048]{1,0:T(8,128)} %get-tuple-element.47) | copy-start | bytes 2359300
  191.7 35.2 %collective-permute-start.29 = (f32[16,2048]{1,0:T(8,128)S(1)}, f32[16,2048]{1,0:T(8,128)S(1)}, u32[]{:S(2)}, u32[]{:S(2)}) collective-permute-start(f32[16,2048]{1,0:T(8,128)S(1)} %get-tuple-element.76), channel_id=1, source_target_pairs={{0,1},{1,0},{2,3},{3,2},{4,5},{5,4},{6,7},{7,6},{8,9},{9,8},{10,11... | collective-permute-start | bytes 393224 | tf_op jit(solution)/shard_map/ppermute | solution.py:53
  195.2 11.6 %collective-permute-start.16 = (f32[48,2048]{1,0:T(8,128)S(1)}, f32[48,2048]{1,0:T(8,128)S(1)}, u32[]{:S(2)}, u32[]{:S(2)}) collective-permute-start(f32[48,2048]{1,0:T(8,128)S(1)} %slice_add_fusion.7), channel_id=1, source_target_pairs={{0,2},{1,3},{2,4},{3,5},{4,6},{5,7},{6,0},{7,1},{8,10},{9,11},{10,... | collective-permute-start | bytes 1179656 | tf_op jit(solution)/shard_map/ppermute | solution.py:53
  203.4 10.4 %collective-permute-start.26 = (f32[48,2048]{1,0:T(8,128)S(1)}, f32[48,2048]{1,0:T(8,128)S(1)}, u32[]{:S(2)}, u32[]{:S(2)}) collective-permute-start(f32[48,2048]{1,0:T(8,128)S(1)} %slice_add_fusion.3), channel_id=1, source_target_pairs={{0,6},{1,7},{2,0},{3,1},{4,2},{5,3},{6,4},{7,5},{8,14},{9,15},{10,... | collective-permute-start | bytes 1179656 | tf_op jit(solution)/shard_map/ppermute | solution.py:53
  206.8 15.1 %copy-start.1 = (f32[96,2048]{1,0:T(8,128)S(1)}, f32[96,2048]{1,0:T(8,128)}, u32[]{:S(2)}) copy-start(f32[96,2048]{1,0:T(8,128)} %get-tuple-element.43) | copy-start | bytes 2359300
  206.9 11.2 %collective-permute-start.10 = (f32[48,2048]{1,0:T(8,128)S(1)}, f32[48,2048]{1,0:T(8,128)S(1)}, u32[]{:S(2)}, u32[]{:S(2)}) collective-permute-start(f32[48,2048]{1,0:T(8,128)S(1)} %slice_add_fusion.9), channel_id=1, source_target_pairs={{0,2},{1,3},{2,4},{3,5},{4,6},{5,7},{6,0},{7,1},{8,10},{9,11},{10,... | collective-permute-start | bytes 1179656 | tf_op jit(solution)/shard_map/ppermute | solution.py:53
  213.8 8.2 %collective-permute-start.24 = (f32[48,2048]{1,0:T(8,128)S(1)}, f32[48,2048]{1,0:T(8,128)S(1)}, u32[]{:S(2)}, u32[]{:S(2)}) collective-permute-start(f32[48,2048]{1,0:T(8,128)S(1)} %slice_add_fusion.5), channel_id=1, source_target_pairs={{0,6},{1,7},{2,0},{3,1},{4,2},{5,3},{6,4},{7,5},{8,14},{9,15},{10,... | collective-permute-start | bytes 1179656 | tf_op jit(solution)/shard_map/ppermute | solution.py:53
  218.1 8.2 %copy-start.13 = (f32[32,2048]{1,0:T(8,128)S(1)}, f32[32,2048]{1,0:T(8,128)}, u32[]{:S(2)}) copy-start(f32[32,2048]{1,0:T(8,128)} %get-tuple-element.39) | copy-start | bytes 786436
  218.1 20.6 %collective-permute-start.27 = (f32[48,2048]{1,0:T(8,128)S(1)}, f32[48,2048]{1,0:T(8,128)S(1)}, u32[]{:S(2)}, u32[]{:S(2)}) collective-permute-start(f32[48,2048]{1,0:T(8,128)S(1)} %get-tuple-element.70), channel_id=1, source_target_pairs={{0,1},{1,0},{2,3},{3,2},{4,5},{5,4},{6,7},{7,6},{8,9},{9,8},{10,11... | collective-permute-start | bytes 1179656 | tf_op jit(solution)/shard_map/ppermute | solution.py:53
  222.8 15.8 %collective-permute-start.25 = (f32[48,2048]{1,0:T(8,128)S(1)}, f32[48,2048]{1,0:T(8,128)S(1)}, u32[]{:S(2)}, u32[]{:S(2)}) collective-permute-start(f32[48,2048]{1,0:T(8,128)S(1)} %get-tuple-element.72), channel_id=1, source_target_pairs={{0,1},{1,0},{2,3},{3,2},{4,5},{5,4},{6,7},{7,6},{8,9},{9,8},{10,11... | collective-permute-start | bytes 1179656 | tf_op jit(solution)/shard_map/ppermute | solution.py:53
  226.9 11.7 %collective-permute-start.23 = (f32[16,2048]{1,0:T(8,128)S(1)}, f32[16,2048]{1,0:T(8,128)S(1)}, u32[]{:S(2)}, u32[]{:S(2)}) collective-permute-start(f32[16,2048]{1,0:T(8,128)S(1)} %get-tuple-element.78), channel_id=1, source_target_pairs={{0,1},{1,0},{2,3},{3,2},{4,5},{5,4},{6,7},{7,6},{8,9},{9,8},{10,11... | collective-permute-start | bytes 393224 | tf_op jit(solution)/shard_map/ppermute | solution.py:53
  226.9 11.7 %copy-start.17 = (f32[16,2048]{1,0:T(8,128)}, f32[16,2048]{1,0:T(8,128)S(1)}, u32[]{:S(2)}) copy-start(f32[16,2048]{1,0:T(8,128)S(1)} %collective-permute-done.29.refs_7_) | copy-start | bytes 393220
  238.6 0.8 copy-start.5
  238.6 0.9 copy-start.6
  245.1 8.4 %collective-permute-start.30 = (f32[1024,512]{1,0:T(8,128)}, f32[1024,512]{1,0:T(8,128)S(1)}, u32[]{:S(2)}, u32[]{:S(2)}) collective-permute-start(f32[1024,512]{1,0:T(8,128)} %get-tuple-element.60), channel_id=1, source_target_pairs={{0,8},{8,0},{16,24},{24,16},{32,40},{40,32},{48,56},{56,48},{64,72... | collective-permute-start | bytes 6291464 | tf_op jit(solution)/shard_map/ppermute | solution.py:53
  253.5 16.3 %copy-start.15 = (f32[128,512]{1,0:T(8,128)S(1)}, f32[128,512]{1,0:T(8,128)}, u32[]{:S(2)}) copy-start(f32[128,512]{1,0:T(8,128)} %get-tuple-element.62) | copy-start | bytes 786436
  253.5 16.3 %copy-start.16 = (f32[128,512]{1,0:T(8,128)S(1)}, f32[128,512]{1,0:T(8,128)}, u32[]{:S(2)}) copy-start(f32[128,512]{1,0:T(8,128)} %get-tuple-element.64) | copy-start | bytes 786436
  255.2 13.2 %collective-permute-start.31 = (f32[256,512]{1,0:T(8,128)S(1)}, f32[256,512]{1,0:T(8,128)S(1)}, u32[]{:S(2)}, u32[]{:S(2)}) collective-permute-start(f32[256,512]{1,0:T(8,128)S(1)} %get-tuple-element.69), channel_id=1, source_target_pairs={{0,6},{1,7},{2,0},{3,1},{4,2},{5,3},{6,4},{7,5},{8,14},{9,15},{10,... | collective-permute-start | bytes 1572872 | tf_op jit(solution)/shard_map/ppermute | solution.py:53
  255.3 14.4 %collective-permute-start.32 = (f32[256,512]{1,0:T(8,128)S(1)}, f32[256,512]{1,0:T(8,128)S(1)}, u32[]{:S(2)}, u32[]{:S(2)}) collective-permute-start(f32[256,512]{1,0:T(8,128)S(1)} %get-tuple-element.68), channel_id=1, source_target_pairs={{0,2},{1,3},{2,4},{3,5},{4,6},{5,7},{6,0},{7,1},{8,10},{9,11},{10,... | collective-permute-start | bytes 1572872 | tf_op jit(solution)/shard_map/ppermute | solution.py:53
  269.9 6.7 %collective-permute-start.34 = (f32[128,512]{1,0:T(8,128)S(1)}, f32[128,512]{1,0:T(8,128)S(1)}, u32[]{:S(2)}, u32[]{:S(2)}) collective-permute-start(f32[128,512]{1,0:T(8,128)S(1)} %get-tuple-element.66), channel_id=1, source_target_pairs={{0,6},{1,7},{2,0},{3,1},{4,2},{5,3},{6,4},{7,5},{8,14},{9,15},{10,... | collective-permute-start | bytes 786440 | tf_op jit(solution)/shard_map/ppermute | solution.py:53
  270.2 9.8 %collective-permute-start.33 = (f32[128,512]{1,0:T(8,128)S(1)}, f32[128,512]{1,0:T(8,128)S(1)}, u32[]{:S(2)}, u32[]{:S(2)}) collective-permute-start(f32[128,512]{1,0:T(8,128)S(1)} %get-tuple-element.65), channel_id=1, source_target_pairs={{0,2},{1,3},{2,4},{3,5},{4,6},{5,7},{6,0},{7,1},{8,10},{9,11},{10,... | collective-permute-start | bytes 786440 | tf_op jit(solution)/shard_map/ppermute | solution.py:53
  276.6 7.8 %collective-permute-start.35 = (f32[128,512]{1,0:T(8,128)S(1)}, f32[128,512]{1,0:T(8,128)S(1)}, u32[]{:S(2)}, u32[]{:S(2)}) collective-permute-start(f32[128,512]{1,0:T(8,128)S(1)} %fusion.4), channel_id=1, source_target_pairs={{0,1},{1,0},{2,3},{3,2},{4,5},{5,4},{6,7},{7,6},{8,9},{9,8},{10,11... | collective-permute-start | bytes 786440 | tf_op jit(solution)/shard_map/ppermute | solution.py:53
  284.6 5.5 %collective-permute-start.36 = (f32[128,512]{1,0:T(8,128)S(1)}, f32[128,512]{1,0:T(8,128)S(1)}, u32[]{:S(2)}, u32[]{:S(2)}) collective-permute-start(f32[128,512]{1,0:T(8,128)S(1)} %fusion.6), channel_id=1, source_target_pairs={{0,64},{8,72},{16,80},{24,88},{32,96},{40,104},{48,112},{56,120},{... | collective-permute-start | bytes 786440 | tf_op jit(solution)/shard_map/ppermute | solution.py:53
  290.1 5.3 %collective-permute-start.37 = (f32[128,512]{1,0:T(8,128)S(1)}, f32[128,512]{1,0:T(8,128)S(1)}, u32[]{:S(2)}, u32[]{:S(2)}) collective-permute-start(f32[128,512]{1,0:T(8,128)S(1)} %add.153), channel_id=1, source_target_pairs={{0,16},{8,24},{16,0},{24,8},{32,48},{40,56},{48,32},{56,40},{64,80... | collective-permute-start | bytes 786440 | tf_op jit(solution)/shard_map/ppermute | solution.py:53
  295.5 6.5 %collective-permute-start.38 = (f32[128,512]{1,0:T(8,128)S(1)}, f32[128,512]{1,0:T(8,128)S(1)}, u32[]{:S(2)}, u32[]{:S(2)}) collective-permute-start(f32[128,512]{1,0:T(8,128)S(1)} %add.154), channel_id=1, source_target_pairs={{0,48},{8,56},{16,32},{24,40},{32,16},{40,24},{48,0},{56,8},{64,11... | collective-permute-start | bytes 786440 | tf_op jit(solution)/shard_map/ppermute | solution.py:53
  302.0 7.2 %collective-permute-start.39 = (f32[128,512]{1,0:T(8,128)S(1)}, f32[128,512]{1,0:T(8,128)S(1)}, u32[]{:S(2)}, u32[]{:S(2)}) collective-permute-start(f32[128,512]{1,0:T(8,128)S(1)} %add.155), channel_id=1, source_target_pairs={{0,8},{8,0},{16,24},{24,16},{32,40},{40,32},{48,56},{56,48},{64,72... | collective-permute-start | bytes 786440 | tf_op jit(solution)/shard_map/ppermute | solution.py:53
  (2 other events, 1.2 us)
